TPU v7x, 32 devices: a whole 2x2x4 slice. The times are simulated.
32 devices in a mesh: grp: 2 (over y), slab: 4 (over z), row: 2 (over x), col: 2 (over core).
Axes of the slice: x: 2, y: 2, z: 4, core: 2. Of those that a mesh axis runs over, the one named last changes fastest.
Arguments:
- image: float32 [3, 64, 32, 256], P(None, ('grp', 'slab'), 'row', 'col'), parts along dimension 1, may hold values from -28 to 28, as said below
- brain_mask: int32 [64, 32, 256], P(('grp', 'slab'), 'row', 'col'), parts along dimension 0, may hold values from 0 to 1, as said below
- labels: int32 [64, 32, 256], P(('grp', 'slab'), 'row', 'col'), parts along dimension 0, may hold values from 0 to 7
Outputs:
- posterior: bfloat16 [8, 64, 32, 256], P(None, ('grp', 'slab'), 'row', 'col'), parts along dimension 1
- bias_field: float32 [3, 64, 32, 256], P(None, ('grp', 'slab'), 'row', 'col'), parts along dimension 1
- class_means: float32 [16, 3], P('grp'), parts along dimension 0
There are 2 independent parts, one for each index of `grp`. A program takes and returns all parts, laid end to end along the dimension named above; each array names one. Nothing has to cross between parts.
Inputs may be any that keep to these rules, and one draw needn't show every extreme that they name: `image`: log intensities of 3 modalities. `brain_mask`: 1 marks a brain cell, 0 a cell outside.
All inputs are finite; a program needn't handle non-finite values.
Results may differ from a plain program's by a relative error of at most 0.001.
Values sent between devices are 32-bit elements; how exact they have to be, the bound alone decides.
A program may use at most 64 MiB of HBM per device.

v0:
```python
import math

import jax
import jax.numpy as jnp
from jax import lax
from jax.sharding import PartitionSpec as P

M = 3
K = 8
EM_ITERS = 2
MF_PASSES = 2


highest = lax.Precision.HIGHEST
coupling = 1.0
breadth = 8.0


def extended(cells, sides, width):
    for axis, dim in sides:
        count = lax.axis_size(axis)
        ends = count - 1
        head = lax.slice_in_dim(cells, 0, width, axis=dim)
        tail = lax.slice_in_dim(cells, cells.shape[dim] - width, cells.shape[dim], axis=dim)
        cells = jnp.concatenate(
            [
                lax.ppermute(tail, axis, [(i, (i + 1) % count) for i in range(ends)]),
                cells,
                lax.ppermute(head, axis, [((i + 1) % count, i) for i in range(ends)]),
            ],
            axis=dim,
        )
    return cells


def circulant(length):
    index = jnp.arange(length, dtype=jnp.int32)
    folded = jnp.minimum(index, length - index).astype(jnp.float32) / length
    response = jnp.exp(-2.0 * math.pi**2 * (length / breadth) ** 2 * folded * folded)
    product = index[:, None] * index[None, :] % length
    angles = 2.0 * math.pi / length * product.astype(jnp.float32)
    cosine = jnp.cos(angles)
    sine = jnp.sin(angles)
    even_part = jnp.dot(cosine * response[None, :], cosine.T, precision=highest)
    odd_part = jnp.dot(sine * response[None, :], sine.T, precision=highest)
    return (even_part + odd_part) / length


def neighbour_sum(belief):
    padded = extended(belief, (("slab", 1), ("row", 2), ("col", 3)), 1)
    total = padded[:, 2:, 1:-1, 1:-1] + padded[:, :-2, 1:-1, 1:-1]
    total = total + padded[:, 1:-1, 2:, 1:-1] + padded[:, 1:-1, :-2, 1:-1]
    total = total + padded[:, 1:-1, 1:-1, 2:] + padded[:, 1:-1, 1:-1, :-2]
    return total


def class_moments(belief, corrected):
    flat = belief.reshape(K, -1)
    values = corrected.reshape(M, -1)
    count, first, squares = lax.psum(
        (
            jnp.sum(flat, axis=1),
            jnp.dot(flat, values.T, precision=highest),
            jnp.dot(flat, (values * values).T, precision=highest),
        ),
        ("slab", "row", "col"),
    )
    means = first / (count + 1.0)[:, None]
    spread = squares - 2.0 * means * first + means * means * count[:, None]
    variance = (spread + 1.0) / (count + 1.0)[:, None]
    return (count, means, variance)


def log_density(corrected, means, variance, prior):
    offset = corrected[None] - means[:, :, None, None, None]
    terms = (
        offset * offset / variance[:, :, None, None, None]
        + jnp.log(variance)[:, :, None, None, None]
    )
    return jnp.log(prior)[:, None, None, None] - 0.5 * jnp.sum(terms, axis=1)


def smoothed(residual, column_local, row_table, slab_table):
    across = jnp.einsum(
        "msrc,cd->msrd",
        lax.all_gather(residual, "col", axis=3, tiled=True),
        column_local,
        precision=highest,
    )
    mixed = jnp.einsum(
        "msrc,rq->msqc",
        lax.all_to_all(across, "row", split_axis=1, concat_axis=2, tiled=True),
        row_table,
        precision=highest,
    )
    across = lax.all_to_all(mixed, "row", split_axis=2, concat_axis=1, tiled=True)
    mixed = jnp.einsum(
        "msrc,sq->mqrc",
        lax.all_to_all(across, "slab", split_axis=2, concat_axis=1, tiled=True),
        slab_table,
        precision=highest,
    )
    return lax.all_to_all(mixed, "slab", split_axis=1, concat_axis=2, tiled=True)


def local(image, brain_mask, labels):
    channels, slabs, rows, columns = image.shape
    inside = brain_mask.astype(jnp.float32)
    kinds = jnp.arange(K, dtype=jnp.int32)
    belief = (labels[None] == kinds[:, None, None, None]).astype(jnp.float32) * inside[None]
    column_table = circulant(columns * lax.axis_size("col"))
    column_local = lax.dynamic_slice_in_dim(
        column_table, lax.axis_index("col") * columns, columns, 1
    )
    row_table = circulant(rows * lax.axis_size("row"))
    slab_table = circulant(slabs * lax.axis_size("slab"))
    bias_field = jnp.zeros_like(image)
    means = jnp.zeros((K, channels), jnp.float32)
    for iteration in range(EM_ITERS):
        corrected = image - bias_field
        count, means, variance = class_moments(belief, corrected)
        prior = (count + 1.0) / (jnp.sum(count) + K)
        total = jnp.sum(belief, axis=0)
        removed = jnp.dot(means.T, belief.reshape(K, -1), precision=highest).reshape(image.shape)
        residual = image * total[None] - removed
        bias_field = smoothed(residual, column_local, row_table, slab_table)
        corrected = image - bias_field
        density = log_density(corrected, means, variance, prior)
        for sweep_index in range(MF_PASSES):
            belief = (
                jax.nn.softmax(density + coupling * neighbour_sum(belief), axis=0) * inside[None]
            )
    return (belief.astype(jnp.bfloat16), bias_field, means)


def solution(mesh):
    placed = (
        P(None, ("grp", "slab"), "row", "col"),
        P(("grp", "slab"), "row", "col"),
        P(("grp", "slab"), "row", "col"),
    )
    return jax.shard_map(
        local,
        mesh=mesh,
        in_specs=placed,
        out_specs=(
            P(None, ("grp", "slab"), "row", "col"),
            P(None, ("grp", "slab"), "row", "col"),
            P("grp", None),
        ),
        check_vma=False,
    )
```

profile of v0, /device:TPU:0, one launch (start us, length us, event | category | flops | bytes accessed | tf_op | source)
XLA Modules:
  0.0 240.6 jit_solution(11587355852781525625)
XLA Ops:
  6.4 35.4 %all-reduce.1 = (f32[8,3]{0,1:T(4,128)S(1)}, f32[8,3]{0,1:T(4,128)S(1)}, f32[8]{0:T(128)S(1)}) all-reduce(f32[8,3]{0,1:T(4,128)S(1)} %fusion.2, f32[8,3]{0,1:T(4,128)S(1)} %convolution_bitcast_fusion.6, f32[8]{0:T(128)S(1)} %select_reduce_fusion), channel_id=1, replica_groups=mesh['grp'=2,'slab'=4,'row'=2,'col'=2] {'slab','row','col'}, use_global_device_ids=true, to_apply=%region_5.6 | all-reduce | flops 56 | bytes 448 | tf_op jit(solution)/shard_map/psum | solution.py:60
  44.3 2.2 all_gather.6
  47.6 3.4 %all-to-all-start = ((f32[3,8,16,128]{3,2,0,1:T(8,128)}), f32[3,8,16,128]{3,2,0,1:T(8,128)S(1)}, u32[]{:S(2)}, u32[]{:S(2)}) async-start(f32[3,8,16,128]{3,2,0,1:T(8,128)} %fusion.39), calls=%async_computation | async-start | bytes 393216 | tf_op jit(solution)/shard_map/all_to_all | solution.py:92
  51.6 4.5 %all-to-all-done = f32[3,8,16,128]{3,2,0,1:T(8,128)S(1)} async-done(((f32[3,8,16,128]{3,2,0,1:T(8,128)}), f32[3,8,16,128]{3,2,0,1:T(8,128)S(1)}, u32[]{:S(2)}, u32[]{:S(2)}) %all-to-all-start) | async-done | bytes 196640 | tf_op jit(solution)/shard_map/all_to_all | solution.py:92
  57.3 3.4 %all-to-all-start.1 = ((f32[3,4,32,128]{3,1,0,2:T(4,128)}), f32[3,4,32,128]{3,1,0,2:T(4,128)S(1)}, u32[]{:S(2)}, u32[]{:S(2)}) async-start(f32[3,4,32,128]{3,1,0,2:T(4,128)} %copy.240), calls=%async_computation.1 | async-start | bytes 393216 | tf_op jit(solution)/shard_map/all_to_all | solution.py:96
  63.3 2.2 all-to-all-done.1
  66.3 3.4 %all-to-all-start.2 = ((f32[3,8,16,128]{3,1,0,2:T(8,128)}), f32[3,8,16,128]{3,1,0,2:T(8,128)S(1)}, u32[]{:S(2)}, u32[]{:S(2)}) async-start(f32[3,8,16,128]{3,1,0,2:T(8,128)} %copy.243), calls=%async_computation.2 | async-start | bytes 393216 | tf_op jit(solution)/shard_map/all_to_all | solution.py:99
  71.1 4.5 %collective-permute-start.3 = (f32[8,10,1,128]{3,0,2,1:T(8,128)S(1)}, f32[8,10,1,128]{3,0,2,1:T(8,128)S(1)}, u32[]{:S(2)}, u32[]{:S(2)}) collective-permute-start(f32[8,10,1,128]{3,0,2,1:T(8,128)S(1)} %copy.339), channel_id=1, source_target_pairs={{0,2},{1,3},{4,6},{5,7},{8,10},{9,11},{12,14},{13,15},{16,18},{17,... | collective-permute-start | bytes 122888 | tf_op jit(solution)/shard_map/ppermute | solution.py:27
  75.7 1.6 collective-permute-done.3
  78.7 5.0 %all-to-all-start.3 = ((f32[3,32,4,128]{3,2,0,1:T(4,128)}), f32[3,32,4,128]{3,2,0,1:T(4,128)S(1)}, u32[]{:S(2)}, u32[]{:S(2)}) async-start(f32[3,32,4,128]{3,2,0,1:T(4,128)} %copy.247), calls=%async_computation.3 | async-start | bytes 393216 | tf_op jit(solution)/shard_map/all_to_all | solution.py:103
  85.0 1.8 copy.258
  92.4 1.6 copy.261
  96.1 3.9 %collective-permute-start.7 = (f32[8,1,16,128]{3,2,1,0:T(8,128)S(1)}, f32[8,1,16,128]{3,2,1,0:T(8,128)S(1)}, u32[]{:S(2)}, u32[]{:S(2)}) collective-permute-start(f32[8,1,16,128]{3,2,1,0:T(8,128)S(1)} %get-tuple-element.53), channel_id=1, source_target_pairs={{0,4},{4,8},{8,12},{1,5},{5,9},{9,13},{2,6},{6,10},{10,14},{3,7},{... | collective-permute-start | bytes 196616 | tf_op jit(solution)/shard_map/ppermute | solution.py:27
  101.9 4.3 %collective-permute-done.6 = f32[8,1,16,128]{3,2,1,0:T(8,128)S(1)} collective-permute-done((f32[8,1,16,128]{3,2,1,0:T(8,128)S(1)}, f32[8,1,16,128]{3,2,1,0:T(8,128)S(1)}, u32[]{:S(2)}, u32[]{:S(2)}) %collective-permute-start.6) | collective-permute-done | bytes 65568 | tf_op jit(solution)/shard_map/ppermute | solution.py:29
  107.6 4.7 %collective-permute-start.9 = (f32[8,10,1,128]{3,0,2,1:T(8,128)S(1)}, f32[8,10,1,128]{3,0,2,1:T(8,128)S(1)}, u32[]{:S(2)}, u32[]{:S(2)}) collective-permute-start(f32[8,10,1,128]{3,0,2,1:T(8,128)S(1)} %copy.341), channel_id=1, source_target_pairs={{0,2},{1,3},{4,6},{5,7},{8,10},{9,11},{12,14},{13,15},{16,18},{17,... | collective-permute-start | bytes 122888 | tf_op jit(solution)/shard_map/ppermute | solution.py:27
  118.0 3.8 %collective-permute-start.11 = (f32[8,10,18,1]{2,0,3,1:T(8,128)S(1)}, f32[8,10,18,1]{2,0,3,1:T(8,128)}, u32[]{:S(2)}, u32[]{:S(2)}) collective-permute-start(f32[8,10,18,1]{2,0,3,1:T(8,128)S(1)} %copy.270), channel_id=1, source_target_pairs={{0,1},{2,3},{4,5},{6,7},{8,9},{10,11},{12,13},{14,15},{16,17},{18,... | collective-permute-start | bytes 17288 | tf_op jit(solution)/shard_map/ppermute | solution.py:27
  128.4 32.9 %all-reduce = (f32[8,3]{0,1:T(4,128)S(1)}, f32[8]{0:T(128)S(1)}, f32[8,3]{0,1:T(4,128)S(1)}) all-reduce(f32[8,3]{0,1:T(4,128)S(1)} %convolution_bitcast_fusion.5, f32[8]{0:T(128)S(1)} %get-tuple-element.10, f32[8,3]{0,1:T(4,128)S(1)} %convolution_bitcast_fusion.4), channel_id=1, replica_groups=mesh['grp'=2,'slab'=4,'row'=2,'col'=2] {'slab','row','col'}, use_global_device_ids=true, to_apply=%region_15.16 | all-reduce | flops 56 | bytes 448 | tf_op jit(solution)/shard_map/psum | solution.py:60
  163.6 2.2 all_gather.7
  166.3 7.4 %all_to_all.144 = f32[3,8,16,128]{3,2,0,1:T(8,128)S(1)} all-to-all(f32[3,8,16,128]{3,2,0,1:T(8,128)S(1)} %fusion.37), channel_id=1, replica_groups=mesh['grp'=2,'slab'=4,'row'=2,'col'=2] {'row'}, dimensions={1} | all-to-all | bytes 393216 | tf_op jit(solution)/shard_map/all_to_all | solution.py:92
  174.9 3.4 %all-to-all-start.5 = ((f32[3,4,32,128]{3,1,0,2:T(4,128)}), f32[3,4,32,128]{3,1,0,2:T(4,128)S(1)}, u32[]{:S(2)}, u32[]{:S(2)}) async-start(f32[3,4,32,128]{3,1,0,2:T(4,128)} %copy.281), calls=%async_computation.5 | async-start | bytes 393216 | tf_op jit(solution)/shard_map/all_to_all | solution.py:96
  180.9 2.2 all-to-all-done.5
  183.9 3.4 %all-to-all-start.6 = ((f32[3,8,16,128]{3,1,0,2:T(8,128)}), f32[3,8,16,128]{3,1,0,2:T(8,128)S(1)}, u32[]{:S(2)}, u32[]{:S(2)}) async-start(f32[3,8,16,128]{3,1,0,2:T(8,128)} %copy.284), calls=%async_computation.6 | async-start | bytes 393216 | tf_op jit(solution)/shard_map/all_to_all | solution.py:99
  188.7 4.5 %collective-permute-start.15 = (f32[8,10,1,128]{3,0,2,1:T(8,128)S(1)}, f32[8,10,1,128]{3,0,2,1:T(8,128)S(1)}, u32[]{:S(2)}, u32[]{:S(2)}) collective-permute-start(f32[8,10,1,128]{3,0,2,1:T(8,128)S(1)} %copy.343), channel_id=1, source_target_pairs={{0,2},{1,3},{4,6},{5,7},{8,10},{9,11},{12,14},{13,15},{16,18},{17,... | collective-permute-start | bytes 122888 | tf_op jit(solution)/shard_map/ppermute | solution.py:27
  193.3 1.6 collective-permute-done.15
  196.3 5.0 %all-to-all-start.7 = ((f32[3,32,4,128]{3,2,0,1:T(4,128)}), f32[3,32,4,128]{3,2,0,1:T(4,128)S(1)}, u32[]{:S(2)}, u32[]{:S(2)}) async-start(f32[3,32,4,128]{3,2,0,1:T(4,128)} %copy.288), calls=%async_computation.7 | async-start | bytes 393216 | tf_op jit(solution)/shard_map/all_to_all | solution.py:103
  202.6 1.8 copy.301
  206.3 3.0 %collective-permute-start.17 = (f32[8,10,18,1]{2,0,3,1:T(8,128)S(1)}, f32[8,10,18,1]{2,0,3,1:T(8,128)S(1)}, u32[]{:S(2)}, u32[]{:S(2)}) collective-permute-start(f32[8,10,18,1]{2,0,3,1:T(8,128)S(1)} %copy.303), channel_id=1, source_target_pairs={{0,1},{2,3},{4,5},{6,7},{8,9},{10,11},{12,13},{14,15},{16,17},{18,... | collective-permute-start | bytes 17288 | tf_op jit(solution)/shard_map/ppermute | solution.py:27
  210.2 1.6 copy.304
  213.9 3.9 %collective-permute-start.19 = (f32[8,1,16,128]{3,2,1,0:T(8,128)S(1)}, f32[8,1,16,128]{3,2,1,0:T(8,128)S(1)}, u32[]{:S(2)}, u32[]{:S(2)}) collective-permute-start(f32[8,1,16,128]{3,2,1,0:T(8,128)S(1)} %get-tuple-element.49), channel_id=1, source_target_pairs={{0,4},{4,8},{8,12},{1,5},{5,9},{9,13},{2,6},{6,10},{10,14},{3,7},{... | collective-permute-start | bytes 196616 | tf_op jit(solution)/shard_map/ppermute | solution.py:27
  219.7 4.3 %collective-permute-done.18 = f32[8,1,16,128]{3,2,1,0:T(8,128)S(1)} collective-permute-done((f32[8,1,16,128]{3,2,1,0:T(8,128)S(1)}, f32[8,1,16,128]{3,2,1,0:T(8,128)S(1)}, u32[]{:S(2)}, u32[]{:S(2)}) %collective-permute-start.18) | collective-permute-done | bytes 65568 | tf_op jit(solution)/shard_map/ppermute | solution.py:29
  225.4 4.8 %collective-permute-start.21 = (f32[8,10,1,128]{3,0,2,1:T(8,128)S(1)}, f32[8,10,1,128]{3,0,2,1:T(8,128)S(1)}, u32[]{:S(2)}, u32[]{:S(2)}) collective-permute-start(f32[8,10,1,128]{3,0,2,1:T(8,128)S(1)} %copy.345), channel_id=1, source_target_pairs={{0,2},{1,3},{4,6},{5,7},{8,10},{9,11},{12,14},{13,15},{16,18},{17,... | collective-permute-start | bytes 122888 | tf_op jit(solution)/shard_map/ppermute | solution.py:27
  234.6 3.0 %collective-permute-start.23 = (f32[8,10,18,1]{2,0,3,1:T(8,128)S(1)}, f32[8,10,18,1]{2,0,3,1:T(8,128)S(1)}, u32[]{:S(2)}, u32[]{:S(2)}) collective-permute-start(f32[8,10,18,1]{2,0,3,1:T(8,128)S(1)} %copy.313), channel_id=1, source_target_pairs={{0,1},{2,3},{4,5},{6,7},{8,9},{10,11},{12,13},{14,15},{16,17},{18,... | collective-permute-start | bytes 17288 | tf_op jit(solution)/shard_map/ppermute | solution.py:27
  (186 shorter events, 67.0 us)
Async XLA Ops:
  47.6 8.5 %all-to-all-start = ((f32[3,8,16,128]{3,2,0,1:T(8,128)}), f32[3,8,16,128]{3,2,0,1:T(8,128)S(1)}, u32[]{:S(2)}, u32[]{:S(2)}) async-start(f32[3,8,16,128]{3,2,0,1:T(8,128)} %fusion.39), calls=%async_computation | async-start | bytes 393216 | tf_op jit(solution)/shard_map/all_to_all | solution.py:92
  57.3 8.2 %all-to-all-start.1 = ((f32[3,4,32,128]{3,1,0,2:T(4,128)}), f32[3,4,32,128]{3,1,0,2:T(4,128)S(1)}, u32[]{:S(2)}, u32[]{:S(2)}) async-start(f32[3,4,32,128]{3,1,0,2:T(4,128)} %copy.240), calls=%async_computation.1 | async-start | bytes 393216 | tf_op jit(solution)/shard_map/all_to_all | solution.py:96
  60.7 8.9 %collective-permute-start.1 = (f32[8,1,16,128]{3,2,1,0:T(8,128)S(1)}, f32[8,1,16,128]{3,2,1,0:T(8,128)S(1)}, u32[]{:S(2)}, u32[]{:S(2)}) collective-permute-start(f32[8,1,16,128]{3,2,1,0:T(8,128)S(1)} %get-tuple-element.55), channel_id=1, source_target_pairs={{0,4},{4,8},{8,12},{1,5},{5,9},{9,13},{2,6},{6,10},{10,14},{3,7},{... | collective-permute-start | bytes 196616 | tf_op jit(solution)/shard_map/ppermute | solution.py:27
  62.0 7.7 %collective-permute-start = (f32[8,1,16,128]{3,2,1,0:T(8,128)S(1)}, f32[8,1,16,128]{3,2,1,0:T(8,128)S(1)}, u32[]{:S(2)}, u32[]{:S(2)}) collective-permute-start(f32[8,1,16,128]{3,2,1,0:T(8,128)S(1)} %get-tuple-element.56), channel_id=1, source_target_pairs={{4,0},{8,4},{12,8},{5,1},{9,5},{13,9},{6,2},{10,6},{14,10},{7,3},{... | collective-permute-start | bytes 196616 | tf_op jit(solution)/shard_map/ppermute | solution.py:29
  66.3 11.2 %all-to-all-start.2 = ((f32[3,8,16,128]{3,1,0,2:T(8,128)}), f32[3,8,16,128]{3,1,0,2:T(8,128)S(1)}, u32[]{:S(2)}, u32[]{:S(2)}) async-start(f32[3,8,16,128]{3,1,0,2:T(8,128)} %copy.243), calls=%async_computation.2 | async-start | bytes 393216 | tf_op jit(solution)/shard_map/all_to_all | solution.py:99
  69.8 5.9 %collective-permute-start.2 = (f32[8,10,1,128]{3,0,2,1:T(8,128)S(1)}, f32[8,10,1,128]{3,0,2,1:T(8,128)S(1)}, u32[]{:S(2)}, u32[]{:S(2)}) collective-permute-start(f32[8,10,1,128]{3,0,2,1:T(8,128)S(1)} %copy.338), channel_id=1, source_target_pairs={{2,0},{3,1},{6,4},{7,5},{10,8},{11,9},{14,12},{15,13},{18,16},{19,... | collective-permute-start | bytes 122888 | tf_op jit(solution)/shard_map/ppermute | solution.py:29
  71.1 6.2 %collective-permute-start.3 = (f32[8,10,1,128]{3,0,2,1:T(8,128)S(1)}, f32[8,10,1,128]{3,0,2,1:T(8,128)S(1)}, u32[]{:S(2)}, u32[]{:S(2)}) collective-permute-start(f32[8,10,1,128]{3,0,2,1:T(8,128)S(1)} %copy.339), channel_id=1, source_target_pairs={{0,2},{1,3},{4,6},{5,7},{8,10},{9,11},{12,14},{13,15},{16,18},{17,... | collective-permute-start | bytes 122888 | tf_op jit(solution)/shard_map/ppermute | solution.py:27
  78.7 15.2 %all-to-all-start.3 = ((f32[3,32,4,128]{3,2,0,1:T(4,128)}), f32[3,32,4,128]{3,2,0,1:T(4,128)S(1)}, u32[]{:S(2)}, u32[]{:S(2)}) async-start(f32[3,32,4,128]{3,2,0,1:T(4,128)} %copy.247), calls=%async_computation.3 | async-start | bytes 393216 | tf_op jit(solution)/shard_map/all_to_all | solution.py:103
  87.4 5.0 %collective-permute-start.5 = (f32[8,10,18,1]{2,0,3,1:T(8,128)S(1)}, f32[8,10,18,1]{2,0,3,1:T(8,128)S(1)}, u32[]{:S(2)}, u32[]{:S(2)}) collective-permute-start(f32[8,10,18,1]{2,0,3,1:T(8,128)S(1)} %copy.260), channel_id=1, source_target_pairs={{0,1},{2,3},{4,5},{6,7},{8,9},{10,11},{12,13},{14,15},{16,17},{18,... | collective-permute-start | bytes 17288 | tf_op jit(solution)/shard_map/ppermute | solution.py:27
  88.7 3.1 %collective-permute-start.4 = (f32[8,10,18,1]{2,0,3,1:T(8,128)S(1)}, f32[8,10,18,1]{2,0,3,1:T(8,128)S(1)}, u32[]{:S(2)}, u32[]{:S(2)}) collective-permute-start(f32[8,10,18,1]{2,0,3,1:T(8,128)S(1)} %copy.258), channel_id=1, source_target_pairs={{1,0},{3,2},{5,4},{7,6},{9,8},{11,10},{13,12},{15,14},{17,16},{19,... | collective-permute-start | bytes 17288 | tf_op jit(solution)/shard_map/ppermute | solution.py:29
  96.1 5.8 %collective-permute-start.7 = (f32[8,1,16,128]{3,2,1,0:T(8,128)S(1)}, f32[8,1,16,128]{3,2,1,0:T(8,128)S(1)}, u32[]{:S(2)}, u32[]{:S(2)}) collective-permute-start(f32[8,1,16,128]{3,2,1,0:T(8,128)S(1)} %get-tuple-element.53), channel_id=1, source_target_pairs={{0,4},{4,8},{8,12},{1,5},{5,9},{9,13},{2,6},{6,10},{10,14},{3,7},{... | collective-permute-start | bytes 196616 | tf_op jit(solution)/shard_map/ppermute | solution.py:27
  100.1 6.2 %collective-permute-start.6 = (f32[8,1,16,128]{3,2,1,0:T(8,128)S(1)}, f32[8,1,16,128]{3,2,1,0:T(8,128)S(1)}, u32[]{:S(2)}, u32[]{:S(2)}) collective-permute-start(f32[8,1,16,128]{3,2,1,0:T(8,128)S(1)} %get-tuple-element.54), channel_id=1, source_target_pairs={{4,0},{8,4},{12,8},{5,1},{9,5},{13,9},{6,2},{10,6},{14,10},{7,3},{... | collective-permute-start | bytes 196616 | tf_op jit(solution)/shard_map/ppermute | solution.py:29
  106.3 6.0 %collective-permute-start.8 = (f32[8,10,1,128]{3,0,2,1:T(8,128)S(1)}, f32[8,10,1,128]{3,0,2,1:T(8,128)S(1)}, u32[]{:S(2)}, u32[]{:S(2)}) collective-permute-start(f32[8,10,1,128]{3,0,2,1:T(8,128)S(1)} %copy.340), channel_id=1, source_target_pairs={{2,0},{3,1},{6,4},{7,5},{10,8},{11,9},{14,12},{15,13},{18,16},{19,... | collective-permute-start | bytes 122888 | tf_op jit(solution)/shard_map/ppermute | solution.py:29
  107.6 6.2 %collective-permute-start.9 = (f32[8,10,1,128]{3,0,2,1:T(8,128)S(1)}, f32[8,10,1,128]{3,0,2,1:T(8,128)S(1)}, u32[]{:S(2)}, u32[]{:S(2)}) collective-permute-start(f32[8,10,1,128]{3,0,2,1:T(8,128)S(1)} %copy.341), channel_id=1, source_target_pairs={{0,2},{1,3},{4,6},{5,7},{8,10},{9,11},{12,14},{13,15},{16,18},{17,... | collective-permute-start | bytes 122888 | tf_op jit(solution)/shard_map/ppermute | solution.py:27
  116.1 5.6 %collective-permute-start.10 = (f32[8,10,18,1]{2,0,3,1:T(8,128)}, f32[8,10,18,1]{2,0,3,1:T(8,128)S(1)}, u32[]{:S(2)}, u32[]{:S(2)}) collective-permute-start(f32[8,10,18,1]{2,0,3,1:T(8,128)} %copy.268), channel_id=1, source_target_pairs={{1,0},{3,2},{5,4},{7,6},{9,8},{11,10},{13,12},{15,14},{17,16},{19,... | collective-permute-start | bytes 17288 | tf_op jit(solution)/shard_map/ppermute | solution.py:29
  118.0 4.4 %collective-permute-start.11 = (f32[8,10,18,1]{2,0,3,1:T(8,128)S(1)}, f32[8,10,18,1]{2,0,3,1:T(8,128)}, u32[]{:S(2)}, u32[]{:S(2)}) collective-permute-start(f32[8,10,18,1]{2,0,3,1:T(8,128)S(1)} %copy.270), channel_id=1, source_target_pairs={{0,1},{2,3},{4,5},{6,7},{8,9},{10,11},{12,13},{14,15},{16,17},{18,... | collective-permute-start | bytes 17288 | tf_op jit(solution)/shard_map/ppermute | solution.py:27
  162.9 46.4 %copy-start.16 = (f32[8,3]{0,1:T(4,128)}, f32[8,3]{0,1:T(4,128)S(1)}, u32[]{:S(2)}) copy-start(f32[8,3]{0,1:T(4,128)S(1)} %get-tuple-element.23) | copy-start | bytes 292
  174.9 8.2 %all-to-all-start.5 = ((f32[3,4,32,128]{3,1,0,2:T(4,128)}), f32[3,4,32,128]{3,1,0,2:T(4,128)S(1)}, u32[]{:S(2)}, u32[]{:S(2)}) async-start(f32[3,4,32,128]{3,1,0,2:T(4,128)} %copy.281), calls=%async_computation.5 | async-start | bytes 393216 | tf_op jit(solution)/shard_map/all_to_all | solution.py:96
  178.3 8.9 %collective-permute-start.13 = (f32[8,1,16,128]{3,2,1,0:T(8,128)S(1)}, f32[8,1,16,128]{3,2,1,0:T(8,128)S(1)}, u32[]{:S(2)}, u32[]{:S(2)}) collective-permute-start(f32[8,1,16,128]{3,2,1,0:T(8,128)S(1)} %get-tuple-element.51), channel_id=1, source_target_pairs={{0,4},{4,8},{8,12},{1,5},{5,9},{9,13},{2,6},{6,10},{10,14},{3,7},{... | collective-permute-start | bytes 196616 | tf_op jit(solution)/shard_map/ppermute | solution.py:27
  179.6 7.7 %collective-permute-start.12 = (f32[8,1,16,128]{3,2,1,0:T(8,128)S(1)}, f32[8,1,16,128]{3,2,1,0:T(8,128)S(1)}, u32[]{:S(2)}, u32[]{:S(2)}) collective-permute-start(f32[8,1,16,128]{3,2,1,0:T(8,128)S(1)} %get-tuple-element.52), channel_id=1, source_target_pairs={{4,0},{8,4},{12,8},{5,1},{9,5},{13,9},{6,2},{10,6},{14,10},{7,3},{... | collective-permute-start | bytes 196616 | tf_op jit(solution)/shard_map/ppermute | solution.py:29
  183.9 11.2 %all-to-all-start.6 = ((f32[3,8,16,128]{3,1,0,2:T(8,128)}), f32[3,8,16,128]{3,1,0,2:T(8,128)S(1)}, u32[]{:S(2)}, u32[]{:S(2)}) async-start(f32[3,8,16,128]{3,1,0,2:T(8,128)} %copy.284), calls=%async_computation.6 | async-start | bytes 393216 | tf_op jit(solution)/shard_map/all_to_all | solution.py:99
  187.4 5.9 %collective-permute-start.14 = (f32[8,10,1,128]{3,0,2,1:T(8,128)S(1)}, f32[8,10,1,128]{3,0,2,1:T(8,128)S(1)}, u32[]{:S(2)}, u32[]{:S(2)}) collective-permute-start(f32[8,10,1,128]{3,0,2,1:T(8,128)S(1)} %copy.342), channel_id=1, source_target_pairs={{2,0},{3,1},{6,4},{7,5},{10,8},{11,9},{14,12},{15,13},{18,16},{19,... | collective-permute-start | bytes 122888 | tf_op jit(solution)/shard_map/ppermute | solution.py:29
  188.7 6.2 %collective-permute-start.15 = (f32[8,10,1,128]{3,0,2,1:T(8,128)S(1)}, f32[8,10,1,128]{3,0,2,1:T(8,128)S(1)}, u32[]{:S(2)}, u32[]{:S(2)}) collective-permute-start(f32[8,10,1,128]{3,0,2,1:T(8,128)S(1)} %copy.343), channel_id=1, source_target_pairs={{0,2},{1,3},{4,6},{5,7},{8,10},{9,11},{12,14},{13,15},{16,18},{17,... | collective-permute-start | bytes 122888 | tf_op jit(solution)/shard_map/ppermute | solution.py:27
  196.3 15.4 %all-to-all-start.7 = ((f32[3,32,4,128]{3,2,0,1:T(4,128)}), f32[3,32,4,128]{3,2,0,1:T(4,128)S(1)}, u32[]{:S(2)}, u32[]{:S(2)}) async-start(f32[3,32,4,128]{3,2,0,1:T(4,128)} %copy.288), calls=%async_computation.7 | async-start | bytes 393216 | tf_op jit(solution)/shard_map/all_to_all | solution.py:103
  204.4 5.2 %collective-permute-start.16 = (f32[8,10,18,1]{2,0,3,1:T(8,128)S(1)}, f32[8,10,18,1]{2,0,3,1:T(8,128)S(1)}, u32[]{:S(2)}, u32[]{:S(2)}) collective-permute-start(f32[8,10,18,1]{2,0,3,1:T(8,128)S(1)} %copy.301), channel_id=1, source_target_pairs={{1,0},{3,2},{5,4},{7,6},{9,8},{11,10},{13,12},{15,14},{17,16},{19,... | collective-permute-start | bytes 17288 | tf_op jit(solution)/shard_map/ppermute | solution.py:29
  206.3 3.9 %collective-permute-start.17 = (f32[8,10,18,1]{2,0,3,1:T(8,128)S(1)}, f32[8,10,18,1]{2,0,3,1:T(8,128)S(1)}, u32[]{:S(2)}, u32[]{:S(2)}) collective-permute-start(f32[8,10,18,1]{2,0,3,1:T(8,128)S(1)} %copy.303), channel_id=1, source_target_pairs={{0,1},{2,3},{4,5},{6,7},{8,9},{10,11},{12,13},{14,15},{16,17},{18,... | collective-permute-start | bytes 17288 | tf_op jit(solution)/shard_map/ppermute | solution.py:27
  213.9 5.8 %collective-permute-start.19 = (f32[8,1,16,128]{3,2,1,0:T(8,128)S(1)}, f32[8,1,16,128]{3,2,1,0:T(8,128)S(1)}, u32[]{:S(2)}, u32[]{:S(2)}) collective-permute-start(f32[8,1,16,128]{3,2,1,0:T(8,128)S(1)} %get-tuple-element.49), channel_id=1, source_target_pairs={{0,4},{4,8},{8,12},{1,5},{5,9},{9,13},{2,6},{6,10},{10,14},{3,7},{... | collective-permute-start | bytes 196616 | tf_op jit(solution)/shard_map/ppermute | solution.py:27
  217.8 6.2 %collective-permute-start.18 = (f32[8,1,16,128]{3,2,1,0:T(8,128)S(1)}, f32[8,1,16,128]{3,2,1,0:T(8,128)S(1)}, u32[]{:S(2)}, u32[]{:S(2)}) collective-permute-start(f32[8,1,16,128]{3,2,1,0:T(8,128)S(1)} %get-tuple-element.50), channel_id=1, source_target_pairs={{4,0},{8,4},{12,8},{5,1},{9,5},{13,9},{6,2},{10,6},{14,10},{7,3},{... | collective-permute-start | bytes 196616 | tf_op jit(solution)/shard_map/ppermute | solution.py:29
  224.1 6.1 %collective-permute-start.20 = (f32[8,10,1,128]{3,0,2,1:T(8,128)S(1)}, f32[8,10,1,128]{3,0,2,1:T(8,128)S(1)}, u32[]{:S(2)}, u32[]{:S(2)}) collective-permute-start(f32[8,10,1,128]{3,0,2,1:T(8,128)S(1)} %copy.344), channel_id=1, source_target_pairs={{2,0},{3,1},{6,4},{7,5},{10,8},{11,9},{14,12},{15,13},{18,16},{19,... | collective-permute-start | bytes 122888 | tf_op jit(solution)/shard_map/ppermute | solution.py:29
  225.4 6.2 %collective-permute-start.21 = (f32[8,10,1,128]{3,0,2,1:T(8,128)S(1)}, f32[8,10,1,128]{3,0,2,1:T(8,128)S(1)}, u32[]{:S(2)}, u32[]{:S(2)}) collective-permute-start(f32[8,10,1,128]{3,0,2,1:T(8,128)S(1)} %copy.345), channel_id=1, source_target_pairs={{0,2},{1,3},{4,6},{5,7},{8,10},{9,11},{12,14},{13,15},{16,18},{17,... | collective-permute-start | bytes 122888 | tf_op jit(solution)/shard_map/ppermute | solution.py:27
  232.7 4.9 %collective-permute-start.22 = (f32[8,10,18,1]{2,0,3,1:T(8,128)S(1)}, f32[8,10,18,1]{2,0,3,1:T(8,128)S(1)}, u32[]{:S(2)}, u32[]{:S(2)}) collective-permute-start(f32[8,10,18,1]{2,0,3,1:T(8,128)S(1)} %copy.311), channel_id=1, source_target_pairs={{1,0},{3,2},{5,4},{7,6},{9,8},{11,10},{13,12},{15,14},{17,16},{19,... | collective-permute-start | bytes 17288 | tf_op jit(solution)/shard_map/ppermute | solution.py:29
  234.6 3.9 %collective-permute-start.23 = (f32[8,10,18,1]{2,0,3,1:T(8,128)S(1)}, f32[8,10,18,1]{2,0,3,1:T(8,128)S(1)}, u32[]{:S(2)}, u32[]{:S(2)}) collective-permute-start(f32[8,10,18,1]{2,0,3,1:T(8,128)S(1)} %copy.313), channel_id=1, source_target_pairs={{0,1},{2,3},{4,5},{6,7},{8,9},{10,11},{12,13},{14,15},{16,17},{18,... | collective-permute-start | bytes 17288 | tf_op jit(solution)/shard_map/ppermute | solution.py:27
  (18 other events, 154.1 us)
where the time goes:
time: 242 us; the launch traced here: 241 us
  starting transfers between devices  82.7 us (34%)
  blocking collectives  80.1 us (33%)
  waiting for transfers between devices  26.4 us (11%)
  local copies, waits for them, and re-layouts  26 us (11%)
  matrix products  12.9 us (5%)
  other arithmetic  9.53 us (4%)
  between operations  2.89 us (1%)
    psum x2, blocking collectives, class_moments(): lax.psum((jnp.sum(flat, axis=1), jnp.dot(flat, values.T, precision=highes...  68.3 us
    ppermute x12, starting transfers between devices, extended(): lax.ppermute(tail, axis, [(i, (i + 1) % count) for i in range(ends)])  40.1 us
    ppermute x12, starting transfers between devices, extended(): lax.ppermute(head, axis, [((i + 1) % count, i) for i in range(ends)])  15.5 us
    ppermute x12, waiting for transfers between devices, extended(): lax.ppermute(head, axis, [((i + 1) % count, i) for i in range(ends)])  10.2 us
    all_to_all x2, starting transfers between devices, smoothed(): lax.all_to_all(mixed, 'slab', split_axis=1, concat_axis=2, tiled=True)  10.1 us
    slice x8, local copies, waits for them, and re-layouts, extended(): head = lax.slice_in_dim(cells, 0, width, axis=dim)  8.48 us
    all_to_all x1, blocking collectives, smoothed(): lax.all_to_all(across, 'row', split_axis=1, concat_axis=2, tiled=True)  7.42 us
    ppermute x12, waiting for transfers between devices, extended(): lax.ppermute(tail, axis, [(i, (i + 1) % count) for i in range(ends)])  7.35 us
  transfers between devices with their start and end apart: 31, of which 13 were waited for; matrix products, arithmetic and copies ran while one was open for 7% of the time, Pallas kernels for 0%

commit v1 on v0

v1 whole, which is shorter than its diff:
```python
import functools
import math

import jax
import jax.numpy as jnp
import numpy as np
from jax import lax
from jax.experimental import pallas as pl
from jax.experimental.pallas import tpu as pltpu
from jax.sharding import PartitionSpec as P

M = 3
K = 8
EM_ITERS = 2
MF_PASSES = 2
STEPS = EM_ITERS * MF_PASSES

MESH = pl.DeviceIdType.MESH
highest = lax.Precision.HIGHEST
coupling = 1.0
breadth = 8.0
f32 = jnp.float32


def response(length):
    folded = np.minimum(np.arange(length), length - np.arange(length)) / length
    return np.exp(-2.0 * np.pi**2 * (length / breadth) ** 2 * folded * folded)


def kernel_of(length):
    return np.real(np.fft.ifft(response(length)))


def column_tables(length):
    resp = response(length)
    kept = [j for j in range(length // 2 + 1) if np.float32(resp[j]) != 0]
    cells = np.arange(length)
    analysis, synthesis = [], []
    for j in kept:
        angle = 2.0 * np.pi * (j * cells % length) / length
        single = j == 0 or 2 * j == length
        weight = (1.0 if single else 2.0) * resp[j] / length
        analysis.append(np.cos(angle))
        synthesis.append(weight * np.cos(angle))
        if not single:
            analysis.append(np.sin(angle))
            synthesis.append(weight * np.sin(angle))
    rows = -(-len(analysis) // 8) * 8
    pad = np.zeros((rows - len(analysis), length))
    return np.concatenate([analysis, pad]), np.concatenate([synthesis, pad])


def row_matrix(nx, slabs, rows):
    line = kernel_of(nx * rows)
    at = np.arange(nx * rows)
    square = line[(at[None, :] - at[:, None]) % (nx * rows)].reshape(nx, rows, nx, rows)
    full = np.einsum("arbq,st->asrbtq", square, np.eye(slabs))
    size = nx * slabs * rows
    return full.reshape(size, size)


def slab_vectors(nz, slabs, rows):
    line = kernel_of(nz * slabs)
    out = np.zeros((nz, slabs, 1, slabs * rows))
    for dz in range(nz):
        for e in range(slabs):
            for s in range(slabs):
                value = line[(slabs * dz + s - (s - e) % slabs) % (nz * slabs)]
                out[dz, e, 0, s * rows : (s + 1) * rows] = value
    return out


def kernel(
    nz, nx, nc, chunk, owners,
    image, mask, labels, ana, syn, rowm, slabv,
    post, bias, means_out,
    bel, colh, cols, rowh, rows_s, corr, dens, res, mom, mom_s, mom_r, par,
    fwd_s, fwd_r, rolled, mixed, back_s, back_r,
    hs_sem, hr_sem, ms_sem, mr_sem, fs_sem, fr_sem, bs_sem, br_sem,
):
    _, S, R, C = image.shape
    count = nz * nx * nc
    z, x, c = lax.axis_index("slab"), lax.axis_index("row"), lax.axis_index("col")
    me = (z * nx + x) * nc + c
    J = ana.shape[1]

    def where_is(q):
        return {"slab": q // (nx * nc), "row": (q // nc) % nx, "col": q % nc}

    def peer(d):
        return lax.rem(me + d, count)

    def source(d):
        return lax.rem(me + count - d, count)

    lane = lax.broadcasted_iota(jnp.int32, (R, C), 1)
    lane3 = lax.broadcasted_iota(jnp.int32, (K, R, C), 2)
    sub3 = lax.broadcasted_iota(jnp.int32, (K, R, C), 1)

    for v in range(STEPS):
        bel[v, :, 0] = jnp.zeros((K, R, C), f32)
        bel[v, :, S + 1] = jnp.zeros((K, R, C), f32)
    rowh[...] = jnp.zeros(rowh.shape, f32)

    barrier = pltpu.get_barrier_semaphore()

    def greet(d, carry):
        pl.semaphore_signal(barrier, inc=1, device_id=where_is(peer(d)), device_id_type=MESH)
        return carry

    lax.fori_loop(1, count, greet, 0)

    def halo_copies(v):
        copies = [
            (z < nz - 1, z > 0, bel.at[v, :, S], bel.at[v, :, 0], {"slab": z + 1}, 0),
            (z > 0, z < nz - 1, bel.at[v, :, 1], bel.at[v, :, S + 1], {"slab": z - 1}, 1),
            (x < nx - 1, x > 0, rows_s.at[v, 1], rowh.at[v, 0], {"row": x + 1}, 2),
            (x > 0, x < nx - 1, rows_s.at[v, 0], rowh.at[v, 1], {"row": x - 1}, 3),
        ]
        if nc == 2:
            copies.append((None, None, cols.at[v], colh.at[v], {"col": 1 - c}, 4))
        out = []
        for sends, receives, src, dst, device, n in copies:
            copy = pltpu.make_async_remote_copy(
                src_ref=src, dst_ref=dst, send_sem=hs_sem.at[v, n], recv_sem=hr_sem.at[v, n],
                device_id=device, device_id_type=MESH,
            )
            out.append((sends, receives, copy))
        return out

    def under(condition, action):
        if condition is None:
            action()
        else:
            pl.when(condition)(action)

    def halo_start(v):
        for sends, _, copy in halo_copies(v):
            under(sends, copy.start)

    def halo_wait(v):
        for _, receives, copy in halo_copies(v):
            under(receives, copy.wait_recv)

    def halo_drain(v):
        for sends, _, copy in halo_copies(v):
            under(sends, copy.wait_send)

    def keep(v, s, block):
        bel[v, :, s + 1] = block
        rows_s[v, 0, s] = block[:, 0]
        rows_s[v, 1, s] = block[:, R - 1]
        if nc == 2:
            packed = jnp.zeros((R, C), f32)
            for k in range(K):
                last = jnp.broadcast_to(block[k, :, C - 1 : C], (R, C))
                first = jnp.broadcast_to(block[k, :, 0:1], (R, C))
                packed = jnp.where(lane == k, jnp.where(c == 0, last, first), packed)
            cols[v, s] = packed

    def begin(s, carry):
        seen = labels[s]
        inside = mask[s].astype(f32)
        block = jnp.stack([jnp.where(seen == k, inside, 0.0) for k in range(K)])
        keep(0, s, block)
        return carry

    lax.fori_loop(0, S, begin, 0)
    pl.semaphore_wait(barrier, count - 1)
    halo_start(0)
    mom[...] = jnp.zeros(mom.shape, f32)

    def exchange_copy(kind, it, d, target, owner):
        if kind == 0:
            src, dst, ss, rs = mom_s.at[it], mom_r.at[it, owner], ms_sem, mr_sem
        elif kind == 1:
            src, dst, ss, rs = fwd_s.at[it, target], fwd_r.at[it, owner], fs_sem, fr_sem
        else:
            src, dst, ss, rs = back_s.at[it, target // nc], back_r.at[it, owner], bs_sem, br_sem
        return pltpu.make_async_remote_copy(
            src_ref=src, dst_ref=dst, send_sem=ss.at[it, d], recv_sem=rs.at[it, d],
            device_id=where_is(target), device_id_type=MESH,
        )

    def each(action):
        def body(d, carry):
            action(d)
            return carry

        lax.fori_loop(1, count, body, 0)

    def moments_out(it):
        for k in range(K):
            weight = bel[it * MF_PASSES, k, 1 : S + 1]
            total = jnp.sum(jnp.sum(weight, axis=0), axis=0, keepdims=True)
            for m in range(M):
                value = corr[m] if it else image[m]
                first = weight * value
                second = first * value
                mom[m * K + k : m * K + k + 1] = total
                at = (M + m) * K + k
                mom[at : at + 1] = jnp.sum(jnp.sum(first, axis=0), axis=0, keepdims=True)
                at = (2 * M + m) * K + k
                mom[at : at + 1] = jnp.sum(jnp.sum(second, axis=0), axis=0, keepdims=True)
        sums = lax.dot_general(
            jnp.ones((8, C), f32), mom[...], (((1,), (1,)), ((), ())),
            precision=highest, preferred_element_type=f32,
        )
        mom_s[it] = sums[0:1]
        each(lambda d: exchange_copy(0, it, d, peer(d), me).start())
        mom_r[it, me] = sums[0:1]

    def moments_in(it):
        each(lambda d: exchange_copy(0, it, d, me, source(d)).wait_recv())
        sums = jnp.broadcast_to(jnp.sum(mom_r[it], axis=0), (8, 128))
        width = M * K
        lanes = lax.broadcasted_iota(jnp.int32, (8, 128), 1)
        counts = sums
        first = pltpu.roll(sums, 128 - width, 1)
        second = pltpu.roll(sums, 128 - 2 * width, 1)
        scale = 1.0 / (counts + 1.0)
        means = first * scale
        spread = second - 2.0 * means * first + means * means * counts
        variance = jnp.where(lanes < width, (spread + 1.0) * scale, 1.0)
        half = 0.5 / variance
        logs = jnp.log(variance)
        everything = jnp.sum(jnp.where(lanes < K, counts, 0.0), axis=1, keepdims=True)
        prior = jnp.where(lanes < K, (counts + 1.0) / (everything + K), 1.0)
        logs_sum = logs
        for m in range(1, M):
            logs_sum = logs_sum + pltpu.roll(logs, 128 - m * K, 1)
        base = jnp.log(prior) - 0.5 * logs_sum
        for n in range(width):
            par[n] = jnp.broadcast_to(means[:, n : n + 1], (8, 128))
            par[width + n] = jnp.broadcast_to(half[:, n : n + 1], (8, 128))
        for k in range(K):
            par[2 * width + k] = jnp.broadcast_to(base[:, k : k + 1], (8, 128))
        if it == EM_ITERS - 1:
            rows = lax.broadcasted_iota(jnp.int32, (8, 128), 0)
            table = jnp.zeros((8, 128), f32)
            for k in range(K):
                for m in range(M):
                    table = jnp.where((rows == k) & (lanes == m), par[m * K + k], table)
            means_out[...] = table[:K, :M]

    def param(n):
        one = par[n, 0:1]
        return jnp.broadcast_to(one, (R, C))

    def residual(it):
        v = it * MF_PASSES

        def body(s, carry):
            block = bel[v, :, s + 1]
            total = jnp.sum(block, axis=0)
            for m in range(M):
                value = image[m, s] * total
                for k in range(K):
                    value = value - block[k] * param(m * K + k)
                res[m, s] = value
            return carry

        lax.fori_loop(0, S, body, 0)

    def smooth(it):
        table = ana[c]
        coefs = [
            lax.dot_general(
                table, res[m].reshape(S * R, C), (((1,), (1,)), ((), ())),
                precision=highest, preferred_element_type=f32,
            )
            for m in range(M)
        ]
        tall = jnp.concatenate(coefs, axis=0)
        spare = owners * chunk - M * J
        if spare:
            tall = jnp.concatenate([tall, jnp.zeros((spare, S * R), f32)], axis=0)
        fwd_s[it] = tall.reshape(owners, chunk, S * R)

        def send(d):
            @pl.when(peer(d) < owners)
            def _():
                exchange_copy(1, it, d, peer(d), me).start()

        each(send)

        @pl.when(me < owners)
        def _():
            fwd_r[it, me] = fwd_s[it, me]
            each(lambda d: exchange_copy(1, it, d, me, source(d)).wait_recv())
            stack = []
            for zz in range(nz):
                across = []
                for xx in range(nx):
                    at = (zz * nx + xx) * nc
                    tile = fwd_r[it, at]
                    for cc in range(1, nc):
                        tile = tile + fwd_r[it, at + cc]
                    across.append(tile)
                stack.append(jnp.concatenate(across, axis=1))
            mixed[...] = jnp.dot(
                jnp.concatenate(stack, axis=0), rowm[...],
                precision=highest, preferred_element_type=f32,
            )
            for xx in range(nx):
                for zz in range(nz):
                    tile = mixed[zz * chunk : (zz + 1) * chunk, xx * S * R : (xx + 1) * S * R]
                    for e in range(S):
                        rolled[zz, e] = pltpu.roll(tile, e * R, 1) if e else tile

                def body(zq, carry):
                    total = jnp.zeros((chunk, S * R), f32)
                    for zz in range(nz):
                        dz = lax.rem(zq + nz - zz, nz)
                        for e in range(S):
                            total = total + rolled[zz, e] * slabv[dz, e]
                    back_s[it, zq * nx + xx] = total
                    return carry

                lax.fori_loop(0, nz, body, 0)
            each(lambda d: exchange_copy(2, it, d, peer(d), me).start())
            back_r[it, me] = back_s[it, me // nc]

        def wait(d):
            @pl.when(source(d) < owners)
            def _():
                exchange_copy(2, it, d, me, source(d)).wait_recv()

        each(wait)
        flat = back_r[it].reshape(owners * chunk, S * R)
        table = syn[c]
        for m in range(M):
            field = lax.dot_general(
                flat[m * J : (m + 1) * J], table, (((0,), (0,)), ((), ())),
                precision=highest, preferred_element_type=f32,
            ).reshape(S, R, C)
            if it == EM_ITERS - 1:
                bias[m] = field
            corr[m] = image[m] - field

    def density():
        width = M * K

        def body(s, carry):
            for k in range(K):
                value = param(2 * width + k)
                for m in range(M):
                    offset = corr[m, s] - param(m * K + k)
                    value = value - offset * offset * param(width + m * K + k)
                dens[k, s] = value
            return carry

        lax.fori_loop(0, S, body, 0)

    def sweep(v):
        edge = jnp.where(c == 0, C - 1, 0)

        def body(s, carry):
            block = bel[v, :, s + 1]
            total = bel[v, :, s] + bel[v, :, s + 2]
            total = total + jnp.where(sub3 == 0, rowh[v, 0, s][:, None, :], pltpu.roll(block, 1, 1))
            total = total + jnp.where(
                sub3 == R - 1, rowh[v, 1, s][:, None, :], pltpu.roll(block, R - 1, 1)
            )
            if nc == 2:
                packed = colh[v, s]
                beyond = jnp.stack(
                    [jnp.broadcast_to(packed[:, k : k + 1], (R, C)) for k in range(K)]
                )
                total = total + jnp.where(lane3 == edge, beyond, 0.0)
            total = total + jnp.where(lane3 == 0, 0.0, pltpu.roll(block, 1, 2))
            total = total + jnp.where(lane3 == C - 1, 0.0, pltpu.roll(block, C - 1, 2))
            logits = dens[:, s] + coupling * total
            powers = jnp.exp(logits - jnp.max(logits, axis=0, keepdims=True))
            scale = mask[s].astype(f32) / jnp.sum(powers, axis=0)
            fresh = powers * scale[None]
            if v == STEPS - 1:
                post[:, s] = fresh.astype(post.dtype)
            else:
                keep(v + 1, s, fresh)
            return carry

        lax.fori_loop(0, S, body, 0)

    for it in range(EM_ITERS):
        moments_out(it)
        moments_in(it)
        residual(it)
        smooth(it)
        density()
        for p in range(MF_PASSES):
            v = it * MF_PASSES + p
            halo_wait(v)
            sweep(v)
            if v < STEPS - 1:
                halo_start(v + 1)

    for v in range(STEPS):
        halo_drain(v)
    for it in range(EM_ITERS):
        def drain(d):
            exchange_copy(0, it, d, peer(d), me).wait_send()

            @pl.when(peer(d) < owners)
            def _():
                exchange_copy(1, it, d, peer(d), me).wait_send()

            @pl.when(me < owners)
            def _():
                exchange_copy(2, it, d, peer(d), me).wait_send()

        each(drain)


def local(nz, nx, nc, image, brain_mask, labels):
    _, S, R, C = image.shape
    count = nz * nx * nc
    analysis, synthesis = column_tables(C * nc)
    J = analysis.shape[0]
    tiles = M * J // 8
    chunk = 8 * -(-tiles // count)
    owners = -(-M * J // chunk)
    ana = jnp.asarray(analysis.reshape(J, nc, C).transpose(1, 0, 2), f32)
    syn = jnp.asarray(synthesis.reshape(J, nc, C).transpose(1, 0, 2), f32)
    rowm = jnp.asarray(row_matrix(nx, S, R), f32)
    slabv = jnp.asarray(slab_vectors(nz, S, R), f32)
    vmem = pl.BlockSpec(memory_space=pltpu.VMEM)
    lanes = S * R
    return pl.pallas_call(
        functools.partial(kernel, nz, nx, nc, chunk, owners),
        out_shape=(
            jax.ShapeDtypeStruct((K, S, R, C), jnp.bfloat16),
            jax.ShapeDtypeStruct((M, S, R, C), f32),
            jax.ShapeDtypeStruct((K, M), f32),
        ),
        in_specs=[vmem] * 7,
        out_specs=(vmem, vmem, vmem),
        scratch_shapes=[
            pltpu.VMEM((STEPS, K, S + 2, R, C), f32),
            pltpu.VMEM((STEPS, S, R, C), f32),
            pltpu.VMEM((STEPS, S, R, C), f32),
            pltpu.VMEM((STEPS, 2, S, K, C), f32),
            pltpu.VMEM((STEPS, 2, S, K, C), f32),
            pltpu.VMEM((M, S, R, C), f32),
            pltpu.VMEM((K, S, R, C), f32),
            pltpu.VMEM((M, S, R, C), f32),
            pltpu.VMEM((128, C), f32),
            pltpu.VMEM((EM_ITERS, 1, 128), f32),
            pltpu.VMEM((EM_ITERS, count, 1, 128), f32),
            pltpu.VMEM((2 * M * K + K, 8, 128), f32),
            pltpu.VMEM((EM_ITERS, owners, chunk, lanes), f32),
            pltpu.VMEM((EM_ITERS, count, chunk, lanes), f32),
            pltpu.VMEM((nz, S, chunk, lanes), f32),
            pltpu.VMEM((nz * chunk, nx * lanes), f32),
            pltpu.VMEM((EM_ITERS, nz * nx, chunk, lanes), f32),
            pltpu.VMEM((EM_ITERS, owners, chunk, lanes), f32),
            pltpu.SemaphoreType.DMA((STEPS, 5)),
            pltpu.SemaphoreType.DMA((STEPS, 5)),
        ]
        + [pltpu.SemaphoreType.DMA((EM_ITERS, count))] * 6,
        compiler_params=pltpu.CompilerParams(
            collective_id=0, has_side_effects=True, vmem_limit_bytes=48 * 1024 * 1024
        ),
    )(image, brain_mask, labels, ana, syn, rowm, slabv)


def solution(mesh):
    placed = (
        P(None, ("grp", "slab"), "row", "col"),
        P(("grp", "slab"), "row", "col"),
        P(("grp", "slab"), "row", "col"),
    )
    return jax.shard_map(
        functools.partial(local, mesh.shape["slab"], mesh.shape["row"], mesh.shape["col"]),
        mesh=mesh,
        in_specs=placed,
        out_specs=(
            P(None, ("grp", "slab"), "row", "col"),
            P(None, ("grp", "slab"), "row", "col"),
            P("grp", None),
        ),
        check_vma=False,
    )
```

time: 242 us -> 62.5 us (0.26)
  starting transfers between devices: 82.7 us -> 0 us
  blocking collectives: 80.1 us -> 0 us
  Pallas kernels: 0 us -> 53.6 us
  waiting for transfers between devices: 26.4 us -> 0 us
  local copies, waits for them, and re-layouts: 26 us -> 7.85 us
  matrix products: 12.9 us -> 0 us
  other arithmetic: 9.53 us -> 0 us
    psum x2 -> x0, blocking collectives: 68.3 us -> none  [class_moments(): lax.psum((jnp.sum(flat, axis=1), jnp.dot(flat, values.T, precision=highes...]
    ppermute x24 -> x0, starting transfers between devices: 55.6 us -> none  [the longest x12 40.1 us: extended(): lax.ppermute(tail, axis, [(i, (i + 1) % count) for i in range(ends)])]
    pallas_call x0 -> x1, Pallas kernels: none -> 53.6 us  [local(): pl.pallas_call(functools.partial(kernel, nz, nx, nc, chunk, owners), out_...]
    all_to_all x7 -> x0, starting transfers between devices: 27.1 us -> none  [the longest x2 10.1 us: smoothed(): lax.all_to_all(mixed, 'slab', split_axis=1, concat_axis=2, tiled=True)]
    ppermute x24 -> x0, waiting for transfers between devices: 17.5 us -> none  [the longest x12 10.2 us: extended(): lax.ppermute(head, axis, [((i + 1) % count, i) for i in range(ends)])]
    dot_general x16 -> x0, matrix products: 12.9 us -> none  [the longest x2 2.73 us: class_moments(): jnp.dot(flat, values.T, precision=highest)]
    slice x16 -> x0, local copies, waits for them, and re-layouts: 10.8 us -> none  [the longest x8 8.48 us: extended(): head = lax.slice_in_dim(cells, 0, width, axis=dim)]
    all_to_all x7 -> x0, waiting for transfers between devices: 8.91 us -> none  [the longest x1 4.53 us: smoothed(): lax.all_to_all(across, 'row', split_axis=1, concat_axis=2, tiled=True)]
  transfers between devices with their start and end apart: 31 -> 0, of which waited for: 13 -> 0; matrix products, arithmetic and copies ran while one was open for 7% -> 0% of each run, Pallas kernels for 0% -> 0%
where the time goes in v1:
time: 62.5 us; the launch traced here: 62.1 us
  Pallas kernels  53.6 us (86%)
  local copies, waits for them, and re-layouts  7.85 us (13%)
  between operations  0.65 us (1%)
    pallas_call x1, Pallas kernels, local(): pl.pallas_call(functools.partial(kernel, nz, nx, nc, chunk, owners), out_...  53.6 us
    unnamed x16, local copies, waits for them, and re-layouts  7.2 us

profile of v1, /device:TPU:0, one launch (start us, length us, event | category | flops | bytes accessed | tf_op | source)
XLA Modules:
  0.0 62.1 jit_solution(4926882473571582098)
XLA Ops:
  0.6 0.0 copy-start
  0.6 0.9 %copy-done = f32[256,256]{1,0:T(8,128)S(1)} copy-done((f32[256,256]{1,0:T(8,128)S(1)}, f32[256,256]{1,0:T(8,128)}, u32[]{:S(2)}) %copy-start) | copy-done | bytes 262168
  1.6 0.0 copy-start.1
  1.6 0.9 %copy-done.1 = f32[3,8,16,128]{3,2,1,0:T(8,128)S(1)} copy-done((f32[3,8,16,128]{3,2,1,0:T(8,128)S(1)}, f32[3,8,16,128]{3,2,1,0:T(8,128)}, u32[]{:S(2)}) %copy-start.1) | copy-done | bytes 196632
  2.5 0.0 copy-start.2
  2.5 0.8 %copy-done.2 = s32[8,16,128]{2,1,0:T(8,128)S(1)} copy-done((s32[8,16,128]{2,1,0:T(8,128)S(1)}, s32[8,16,128]{2,1,0:T(8,128)}, u32[]{:S(2)}) %copy-start.2) | copy-done | bytes 65560
  3.4 0.0 copy-start.3
  3.4 0.8 %copy-done.3 = s32[8,16,128]{2,1,0:T(8,128)S(1)} copy-done((s32[8,16,128]{2,1,0:T(8,128)S(1)}, s32[8,16,128]{2,1,0:T(8,128)}, u32[]{:S(2)}) %copy-start.3) | copy-done | bytes 65560
  4.2 0.0 copy-start.4
  4.2 0.8 %copy-done.4 = f32[2,40,128]{2,1,0:T(8,128)S(1)} copy-done((f32[2,40,128]{2,1,0:T(8,128)S(1)}, f32[2,40,128]{2,1,0:T(8,128)}, u32[]{:S(2)}) %copy-start.4) | copy-done | bytes 40984
  5.0 0.0 copy-start.5
  5.0 0.8 %copy-done.5 = f32[2,40,128]{2,1,0:T(8,128)S(1)} copy-done((f32[2,40,128]{2,1,0:T(8,128)S(1)}, f32[2,40,128]{2,1,0:T(8,128)}, u32[]{:S(2)}) %copy-start.5) | copy-done | bytes 40984
  5.7 0.0 copy-start.6
  5.8 0.7 %copy-done.6 = f32[4,8,1,128]{3,2,1,0:T(1,128)S(1)} copy-done((f32[4,8,1,128]{3,2,1,0:T(1,128)S(1)}, f32[4,8,1,128]{3,2,1,0:T(1,128)}, u32[]{:S(2)}) %copy-start.6) | copy-done | bytes 16408
  6.5 53.6 %shard_map.94 = (bf16[8,8,16,128]{3,2,1,0:T(8,128)(2,1)S(1)}, f32[3,8,16,128]{3,2,1,0:T(8,128)S(1)}, f32[8,3]{1,0:T(8,128)S(1)}) custom-call(f32[3,8,16,128]{3,2,1,0:T(8,128)S(1)} %copy-done.1, s32[8,16,128]{2,1,0:T(8,128)S(1)} %copy-done.2, s32[8,16,128]{2,1,0:T(8,128)S(1)} %copy-done.3, f32[2,40,128]{2,1,0:T(8,128)S(1)} %copy-done.5, ...), custom_call_target="tpu_custom_call" | custom-call | tf_op jit(solution)/shard_map/pallas_call | solution.py:429
  60.0 0.7 %copy.10 = f32[8,3]{0,1:T(4,128)} copy(f32[8,3]{1,0:T(8,128)S(1)} %get-tuple-element.5) | data formatting | bytes 192 | tf_op jit(solution)/shard_map/pallas_call | solution.py:429
  60.7 0.7 %copy.13 = bf16[8,8,16,128]{3,2,1,0:T(8,128)(2,1)} copy(bf16[8,8,16,128]{3,2,1,0:T(8,128)(2,1)S(1)} %get-tuple-element.9) | data formatting | bytes 524288
  61.4 0.7 %copy.14 = f32[3,8,16,128]{3,2,1,0:T(8,128)} copy(f32[3,8,16,128]{3,2,1,0:T(8,128)S(1)} %get-tuple-element.10) | data formatting | bytes 393216
Async XLA Ops:
  0.6 1.0 %copy-start = (f32[256,256]{1,0:T(8,128)S(1)}, f32[256,256]{1,0:T(8,128)}, u32[]{:S(2)}) copy-start(f32[256,256]{1,0:T(8,128)} %constant.10.clone.rowm) | copy-start | bytes 786436
  1.6 0.9 %copy-start.1 = (f32[3,8,16,128]{3,2,1,0:T(8,128)S(1)}, f32[3,8,16,128]{3,2,1,0:T(8,128)}, u32[]{:S(2)}) copy-start(f32[3,8,16,128]{3,2,1,0:T(8,128)} %image.1) | copy-start | bytes 589828
  2.5 0.8 %copy-start.2 = (s32[8,16,128]{2,1,0:T(8,128)S(1)}, s32[8,16,128]{2,1,0:T(8,128)}, u32[]{:S(2)}) copy-start(s32[8,16,128]{2,1,0:T(8,128)} %mask.1) | copy-start | bytes 196612
  3.4 0.8 %copy-start.3 = (s32[8,16,128]{2,1,0:T(8,128)S(1)}, s32[8,16,128]{2,1,0:T(8,128)}, u32[]{:S(2)}) copy-start(s32[8,16,128]{2,1,0:T(8,128)} %labels.1) | copy-start | bytes 196612
  4.2 0.8 %copy-start.4 = (f32[2,40,128]{2,1,0:T(8,128)S(1)}, f32[2,40,128]{2,1,0:T(8,128)}, u32[]{:S(2)}) copy-start(f32[2,40,128]{2,1,0:T(8,128)} %constant.9.clone.syn) | copy-start | bytes 122884
  5.0 0.8 %copy-start.5 = (f32[2,40,128]{2,1,0:T(8,128)S(1)}, f32[2,40,128]{2,1,0:T(8,128)}, u32[]{:S(2)}) copy-start(f32[2,40,128]{2,1,0:T(8,128)} %constant.8.clone.ana) | copy-start | bytes 122884
  5.7 0.7 %copy-start.6 = (f32[4,8,1,128]{3,2,1,0:T(1,128)S(1)}, f32[4,8,1,128]{3,2,1,0:T(1,128)}, u32[]{:S(2)}) copy-start(f32[4,8,1,128]{3,2,1,0:T(1,128)} %constant.11.clone.slabv) | copy-start | bytes 49156

commit v2 on v1

--- a/solution.py
+++ b/solution.py
@@ -72,26 +72,52 @@
 
 def kernel(
     nz, nx, nc, chunk, owners,
+    image_h, mask_h, labels_h, ana_h, syn_h, rowm_h, slabv_h,
+    post, bias, means_out,
     image, mask, labels, ana, syn, rowm, slabv,
-    post, bias, means_out,
     bel, colh, cols, rowh, rows_s, corr, dens, res, mom, mom_s, mom_r, par,
     fwd_s, fwd_r, rolled, mixed, back_s, back_r,
-    hs_sem, hr_sem, ms_sem, mr_sem, fs_sem, fr_sem, bs_sem, br_sem,
+    hs_sem, hr_sem, ms_sem, mr_sem, fs_sem, fr_sem, bs_sem, br_sem, in_sem,
 ):
     _, S, R, C = image.shape
     count = nz * nx * nc
     z, x, c = lax.axis_index("slab"), lax.axis_index("row"), lax.axis_index("col")
     me = (z * nx + x) * nc + c
-    J = ana.shape[1]
-
-    def where_is(q):
-        return {"slab": q // (nx * nc), "row": (q // nc) % nx, "col": q % nc}
-
-    def peer(d):
-        return lax.rem(me + d, count)
-
-    def source(d):
-        return lax.rem(me + count - d, count)
+    J = ana.shape[0]
+    everyone = owners == count
+
+    fetches = [
+        pltpu.make_async_copy(src, dst, in_sem.at[n])
+        for n, (src, dst) in enumerate(
+            [
+                (labels_h, labels), (mask_h, mask), (image_h, image), (ana_h.at[c], ana),
+                (rowm_h, rowm), (slabv_h, slabv), (syn_h.at[c], syn),
+            ]
+        )
+    ]
+    for fetch in fetches:
+        fetch.start()
+
+    def moved(at, by, size):
+        if size == 1:
+            return at
+        there = at + by
+        return jnp.where(there >= size, there - size, there)
+
+    def shifted(dz, dx, dc):
+        zz, xx, cc = moved(z, dz, nz), moved(x, dx, nx), moved(c, dc, nc)
+        return {"slab": zz, "row": xx, "col": cc}, (zz * nx + xx) * nc + cc
+
+    def each(action):
+        if count <= 32:
+            for d in range(count - 1, 0, -1):
+                action(*shifted(d // (nx * nc), d // nc % nx, d % nc))
+        else:
+            def body(d, carry):
+                action(*shifted(d // (nx * nc), d // nc % nx, d % nc))
+                return carry
+
+            lax.fori_loop(1, count, body, 0)
 
     lane = lax.broadcasted_iota(jnp.int32, (R, C), 1)
     lane3 = lax.broadcasted_iota(jnp.int32, (K, R, C), 2)
@@ -104,11 +130,11 @@
 
     barrier = pltpu.get_barrier_semaphore()
 
-    def greet(d, carry):
-        pl.semaphore_signal(barrier, inc=1, device_id=where_is(peer(d)), device_id_type=MESH)
-        return carry
-
-    lax.fori_loop(1, count, greet, 0)
+    each(
+        lambda device, q: pl.semaphore_signal(
+            barrier, inc=1, device_id=device, device_id_type=MESH
+        )
+    )
 
     def halo_copies(v):
         copies = [
@@ -134,8 +160,8 @@
         else:
             pl.when(condition)(action)
 
-    def halo_start(v):
-        for sends, _, copy in halo_copies(v):
+    def halo_start(v, first=0, last=5):
+        for sends, _, copy in halo_copies(v)[first:last]:
             under(sends, copy.start)
 
     def halo_wait(v):
@@ -165,29 +191,21 @@
         keep(0, s, block)
         return carry
 
+    fetches[0].wait()
+    fetches[1].wait()
     lax.fori_loop(0, S, begin, 0)
-    pl.semaphore_wait(barrier, count - 1)
-    halo_start(0)
     mom[...] = jnp.zeros(mom.shape, f32)
-
-    def exchange_copy(kind, it, d, target, owner):
-        if kind == 0:
-            src, dst, ss, rs = mom_s.at[it], mom_r.at[it, owner], ms_sem, mr_sem
-        elif kind == 1:
-            src, dst, ss, rs = fwd_s.at[it, target], fwd_r.at[it, owner], fs_sem, fr_sem
-        else:
-            src, dst, ss, rs = back_s.at[it, target // nc], back_r.at[it, owner], bs_sem, br_sem
-        return pltpu.make_async_remote_copy(
-            src_ref=src, dst_ref=dst, send_sem=ss.at[it, d], recv_sem=rs.at[it, d],
-            device_id=where_is(target), device_id_type=MESH,
-        )
-
-    def each(action):
-        def body(d, carry):
-            action(d)
-            return carry
-
-        lax.fori_loop(1, count, body, 0)
+    fetches[2].wait()
+
+    def send(src, dst, send_sem, recv_sem, device):
+        pltpu.make_async_remote_copy(
+            src_ref=src, dst_ref=dst, send_sem=send_sem, recv_sem=recv_sem,
+            device_id=device, device_id_type=MESH,
+        ).start()
+
+    def await_bytes(buffer, n, sem):
+        whole = buffer.at[pl.ds(0, n)]
+        pltpu.make_async_copy(whole, whole, sem).wait()
 
     def moments_out(it):
         for k in range(K):
@@ -207,11 +225,18 @@
             precision=highest, preferred_element_type=f32,
         )
         mom_s[it] = sums[0:1]
-        each(lambda d: exchange_copy(0, it, d, peer(d), me).start())
+        if it == 0:
+            pl.semaphore_wait(barrier, count - 1)
+        each(
+            lambda device, q: send(
+                mom_s.at[it], mom_r.at[it, me], ms_sem.at[it], mr_sem.at[it], device
+            )
+        )
+        halo_start(it * MF_PASSES)
         mom_r[it, me] = sums[0:1]
 
     def moments_in(it):
-        each(lambda d: exchange_copy(0, it, d, me, source(d)).wait_recv())
+        await_bytes(mom_r.at[it], count - 1, mr_sem.at[it])
         sums = jnp.broadcast_to(jnp.sum(mom_r[it], axis=0), (8, 128))
         width = M * K
         lanes = lax.broadcasted_iota(jnp.int32, (8, 128), 1)
@@ -263,7 +288,9 @@
         lax.fori_loop(0, S, body, 0)
 
     def smooth(it):
-        table = ana[c]
+        if it == 0:
+            fetches[3].wait()
+        table = ana[...]
         coefs = [
             lax.dot_general(
                 table, res[m].reshape(S * R, C), (((1,), (1,)), ((), ())),
@@ -277,17 +304,20 @@
             tall = jnp.concatenate([tall, jnp.zeros((spare, S * R), f32)], axis=0)
         fwd_s[it] = tall.reshape(owners, chunk, S * R)
 
-        def send(d):
-            @pl.when(peer(d) < owners)
-            def _():
-                exchange_copy(1, it, d, peer(d), me).start()
-
-        each(send)
-
-        @pl.when(me < owners)
-        def _():
+        def forward(device, q):
+            def go():
+                send(fwd_s.at[it, q], fwd_r.at[it, me], fs_sem.at[it], fr_sem.at[it], device)
+
+            under(None if everyone else q < owners, go)
+
+        each(forward)
+        if it == 0:
+            fetches[4].wait()
+            fetches[5].wait()
+
+        def own():
             fwd_r[it, me] = fwd_s[it, me]
-            each(lambda d: exchange_copy(1, it, d, me, source(d)).wait_recv())
+            await_bytes(fwd_r.at[it], count - 1, fr_sem.at[it])
             stack = []
             for zz in range(nz):
                 across = []
@@ -318,17 +348,23 @@
                     return carry
 
                 lax.fori_loop(0, nz, body, 0)
-            each(lambda d: exchange_copy(2, it, d, peer(d), me).start())
+            each(
+                lambda device, q: send(
+                    back_s.at[it, q // nc], back_r.at[it, me], bs_sem.at[it], br_sem.at[it], device
+                )
+            )
             back_r[it, me] = back_s[it, me // nc]
 
-        def wait(d):
-            @pl.when(source(d) < owners)
-            def _():
-                exchange_copy(2, it, d, me, source(d)).wait_recv()
-
-        each(wait)
+        under(None if everyone else me < owners, own)
+        if it == 0:
+            fetches[6].wait()
+        if everyone:
+            await_bytes(back_r.at[it], owners - 1, br_sem.at[it])
+        else:
+            under(me < owners, lambda: await_bytes(back_r.at[it], owners - 1, br_sem.at[it]))
+            under(me >= owners, lambda: await_bytes(back_r.at[it], owners, br_sem.at[it]))
         flat = back_r[it].reshape(owners * chunk, S * R)
-        table = syn[c]
+        table = syn[...]
         for m in range(M):
             field = lax.dot_general(
                 flat[m * J : (m + 1) * J], table, (((0,), (0,)), ((), ())),
@@ -380,7 +416,12 @@
                 keep(v + 1, s, fresh)
             return carry
 
-        lax.fori_loop(0, S, body, 0)
+        lax.fori_loop(0, 2, lambda i, carry: body(i * (S - 1), carry), 0)
+        if v % MF_PASSES < MF_PASSES - 1:
+            halo_start(v + 1, 0, 2)
+        lax.fori_loop(1, S - 1, body, 0)
+        if v % MF_PASSES < MF_PASSES - 1:
+            halo_start(v + 1, 2, 5)
 
     for it in range(EM_ITERS):
         moments_out(it)
@@ -392,24 +433,23 @@
             v = it * MF_PASSES + p
             halo_wait(v)
             sweep(v)
-            if v < STEPS - 1:
-                halo_start(v + 1)
 
     for v in range(STEPS):
         halo_drain(v)
     for it in range(EM_ITERS):
-        def drain(d):
-            exchange_copy(0, it, d, peer(d), me).wait_send()
-
-            @pl.when(peer(d) < owners)
-            def _():
-                exchange_copy(1, it, d, peer(d), me).wait_send()
-
-            @pl.when(me < owners)
-            def _():
-                exchange_copy(2, it, d, peer(d), me).wait_send()
-
-        each(drain)
+        await_bytes(mom_r.at[it], count - 1, ms_sem.at[it])
+        if everyone:
+            await_bytes(fwd_r.at[it], owners - 1, fs_sem.at[it])
+            await_bytes(fwd_r.at[it], count - 1, bs_sem.at[it])
+        else:
+            under(me >= owners, lambda: await_bytes(fwd_r.at[it], owners, fs_sem.at[it]))
+
+            def drain():
+                if owners > 1:
+                    await_bytes(fwd_r.at[it], owners - 1, fs_sem.at[it])
+                await_bytes(fwd_r.at[it], count - 1, bs_sem.at[it])
+
+            under(me < owners, drain)
 
 
 def local(nz, nx, nc, image, brain_mask, labels):
@@ -420,6 +460,8 @@
     tiles = M * J // 8
     chunk = 8 * -(-tiles // count)
     owners = -(-M * J // chunk)
+    if count <= 2 * owners:
+        owners = count
     ana = jnp.asarray(analysis.reshape(J, nc, C).transpose(1, 0, 2), f32)
     syn = jnp.asarray(synthesis.reshape(J, nc, C).transpose(1, 0, 2), f32)
     rowm = jnp.asarray(row_matrix(nx, S, R), f32)
@@ -433,9 +475,16 @@
             jax.ShapeDtypeStruct((M, S, R, C), f32),
             jax.ShapeDtypeStruct((K, M), f32),
         ),
-        in_specs=[vmem] * 7,
+        in_specs=[pl.BlockSpec(memory_space=pl.ANY)] * 7,
         out_specs=(vmem, vmem, vmem),
         scratch_shapes=[
+            pltpu.VMEM((M, S, R, C), f32),
+            pltpu.VMEM((S, R, C), jnp.int32),
+            pltpu.VMEM((S, R, C), jnp.int32),
+            pltpu.VMEM((J, C), f32),
+            pltpu.VMEM((J, C), f32),
+            pltpu.VMEM(rowm.shape, f32),
+            pltpu.VMEM(slabv.shape, f32),
             pltpu.VMEM((STEPS, K, S + 2, R, C), f32),
             pltpu.VMEM((STEPS, S, R, C), f32),
             pltpu.VMEM((STEPS, S, R, C), f32),
@@ -457,9 +506,10 @@
             pltpu.SemaphoreType.DMA((STEPS, 5)),
             pltpu.SemaphoreType.DMA((STEPS, 5)),
         ]
-        + [pltpu.SemaphoreType.DMA((EM_ITERS, count))] * 6,
+        + [pltpu.SemaphoreType.DMA((EM_ITERS,))] * 6
+        + [pltpu.SemaphoreType.DMA((7,))],
         compiler_params=pltpu.CompilerParams(
-            collective_id=0, has_side_effects=True, vmem_limit_bytes=48 * 1024 * 1024
+            collective_id=0, has_side_effects=True, vmem_limit_bytes=65400 * 1024
         ),
     )(image, brain_mask, labels, ana, syn, rowm, slabv)
 

time: 62.5 us -> 55.9 us (0.89)
  local copies, waits for them, and re-layouts: 7.85 us -> 3.71 us
  Pallas kernels: 53.6 us -> 51.3 us
    unnamed x16 -> x6, local copies, waits for them, and re-layouts: 7.2 us -> 3.06 us
    pallas_call x1, Pallas kernels: 53.6 us -> 51.3 us  [local(): pl.pallas_call(functools.partial(kernel, nz, nx, nc, chunk, owners), out_...]
where the time goes in v2:
time: 55.9 us; the launch traced here: 55.7 us
  Pallas kernels  51.3 us (92%)
  local copies, waits for them, and re-layouts  3.71 us (7%)
  between operations  0.65 us (1%)
    pallas_call x1, Pallas kernels, local(): pl.pallas_call(functools.partial(kernel, nz, nx, nc, chunk, owners), out_...  51.3 us
    unnamed x6, local copies, waits for them, and re-layouts  3.06 us

profile of v2, /device:TPU:0, one launch (start us, length us, event | category | flops | bytes accessed | tf_op | source)
XLA Modules:
  0.0 55.7 jit_solution(13293218021952620699)
XLA Ops:
  0.6 51.3 %shard_map.94 = (bf16[8,8,16,128]{3,2,1,0:T(8,128)(2,1)}, f32[3,8,16,128]{3,2,1,0:T(8,128)}, f32[8,3]{1,0:T(8,128)}) custom-call(f32[3,8,16,128]{3,2,1,0:T(8,128)} %image_h.1, s32[8,16,128]{2,1,0:T(8,128)} %mask_h.1, s32[8,16,128]{2,1,0:T(8,128)} %labels_h.1, f32[2,40,128]{2,1,0:T(8,128)} %constant.8.clone.ana_h, f32[2,40,128]{2,1,0:T(8,128)} %constant.9.clone.syn_h, ...), custom_call_target="tpu_custom_call" | custom-call | tf_op jit(solution)/shard_map/pallas_call | solution.py:471
  52.0 0.0 copy-start.1
  52.0 0.7 %copy-done.1 = f32[8,3]{1,0:T(8,128)S(1)} copy-done((f32[8,3]{1,0:T(8,128)S(1)}, f32[8,3]{1,0:T(8,128)}, u32[]{:S(2)}) %copy-start.1) | copy-done | bytes 120
  52.6 0.7 %copy.10 = f32[8,3]{0,1:T(4,128)} copy(f32[8,3]{1,0:T(8,128)S(1)} %copy-done.1) | data formatting | bytes 192 | tf_op jit(solution)/shard_map/pallas_call | solution.py:471
  53.3 0.0 copy-start
  53.3 1.7 %copy.13 = bf16[8,8,16,128]{3,2,1,0:T(8,128)(2,1)} copy(bf16[8,8,16,128]{3,2,1,0:T(8,128)(2,1)} %get-tuple-element.9) | data formatting | bytes 524288
  55.0 0.0 copy-done
  55.0 0.7 %copy.14 = f32[3,8,16,128]{3,2,1,0:T(8,128)} copy(f32[3,8,16,128]{3,2,1,0:T(8,128)S(1)} %copy-done) | data formatting | bytes 393216
Async XLA Ops:
  52.0 0.7 %copy-start.1 = (f32[8,3]{1,0:T(8,128)S(1)}, f32[8,3]{1,0:T(8,128)}, u32[]{:S(2)}) copy-start(f32[8,3]{1,0:T(8,128)} %get-tuple-element.5) | copy-start | bytes 292
  53.3 1.7 %copy-start = (f32[3,8,16,128]{3,2,1,0:T(8,128)S(1)}, f32[3,8,16,128]{3,2,1,0:T(8,128)}, u32[]{:S(2)}) copy-start(f32[3,8,16,128]{3,2,1,0:T(8,128)} %get-tuple-element.10) | copy-start | bytes 589828

commit v3 on v2

--- a/solution.py
+++ b/solution.py
@@ -193,7 +193,7 @@
 
     fetches[0].wait()
     fetches[1].wait()
-    lax.fori_loop(0, S, begin, 0)
+    lax.fori_loop(0, S, begin, 0, unroll=True)
     mom[...] = jnp.zeros(mom.shape, f32)
     fetches[2].wait()
 
@@ -285,7 +285,7 @@
                 res[m, s] = value
             return carry
 
-        lax.fori_loop(0, S, body, 0)
+        lax.fori_loop(0, S, body, 0, unroll=True)
 
     def smooth(it):
         if it == 0:
@@ -347,7 +347,7 @@
                     back_s[it, zq * nx + xx] = total
                     return carry
 
-                lax.fori_loop(0, nz, body, 0)
+                lax.fori_loop(0, nz, body, 0, unroll=nz <= 4)
             each(
                 lambda device, q: send(
                     back_s.at[it, q // nc], back_r.at[it, me], bs_sem.at[it], br_sem.at[it], device
@@ -386,7 +386,7 @@
                 dens[k, s] = value
             return carry
 
-        lax.fori_loop(0, S, body, 0)
+        lax.fori_loop(0, S, body, 0, unroll=True)
 
     def sweep(v):
         edge = jnp.where(c == 0, C - 1, 0)
@@ -416,10 +416,11 @@
                 keep(v + 1, s, fresh)
             return carry
 
-        lax.fori_loop(0, 2, lambda i, carry: body(i * (S - 1), carry), 0)
+        body(0, 0)
+        body(S - 1, 0)
         if v % MF_PASSES < MF_PASSES - 1:
             halo_start(v + 1, 0, 2)
-        lax.fori_loop(1, S - 1, body, 0)
+        lax.fori_loop(1, S - 1, body, 0, unroll=True)
         if v % MF_PASSES < MF_PASSES - 1:
             halo_start(v + 1, 2, 5)
 

time: 55.9 us -> 52 us (0.930)
  Pallas kernels: 51.3 us -> 47.4 us
    pallas_call x1, Pallas kernels: 51.3 us -> 47.4 us  [local(): pl.pallas_call(functools.partial(kernel, nz, nx, nc, chunk, owners), out_...]
where the time goes in v3:
time: 52 us; the launch traced here: 51.8 us
  Pallas kernels  47.4 us (91%)
  local copies, waits for them, and re-layouts  3.71 us (7%)
  between operations  0.65 us (1%)
    pallas_call x1, Pallas kernels, local(): pl.pallas_call(functools.partial(kernel, nz, nx, nc, chunk, owners), out_...  47.4 us
    unnamed x6, local copies, waits for them, and re-layouts  3.06 us

profile of v3, /device:TPU:0, one launch (start us, length us, event | category | flops | bytes accessed | tf_op | source)
XLA Modules:
  0.0 51.8 jit_solution(511410151489915554)
XLA Ops:
  0.6 47.4 %shard_map.94 = (bf16[8,8,16,128]{3,2,1,0:T(8,128)(2,1)}, f32[3,8,16,128]{3,2,1,0:T(8,128)}, f32[8,3]{1,0:T(8,128)}) custom-call(f32[3,8,16,128]{3,2,1,0:T(8,128)} %image_h.1, s32[8,16,128]{2,1,0:T(8,128)} %mask_h.1, s32[8,16,128]{2,1,0:T(8,128)} %labels_h.1, f32[2,40,128]{2,1,0:T(8,128)} %constant.8.clone.ana_h, f32[2,40,128]{2,1,0:T(8,128)} %constant.9.clone.syn_h, ...), custom_call_target="tpu_custom_call" | custom-call | tf_op jit(solution)/shard_map/pallas_call | solution.py:472
  48.1 0.0 copy-start.1
  48.1 0.7 %copy-done.1 = f32[8,3]{1,0:T(8,128)S(1)} copy-done((f32[8,3]{1,0:T(8,128)S(1)}, f32[8,3]{1,0:T(8,128)}, u32[]{:S(2)}) %copy-start.1) | copy-done | bytes 120
  48.7 0.7 %copy.10 = f32[8,3]{0,1:T(4,128)} copy(f32[8,3]{1,0:T(8,128)S(1)} %copy-done.1) | data formatting | bytes 192 | tf_op jit(solution)/shard_map/pallas_call | solution.py:472
  49.4 0.0 copy-start
  49.4 1.7 %copy.13 = bf16[8,8,16,128]{3,2,1,0:T(8,128)(2,1)} copy(bf16[8,8,16,128]{3,2,1,0:T(8,128)(2,1)} %get-tuple-element.9) | data formatting | bytes 524288
  51.1 0.0 copy-done
  51.1 0.7 %copy.14 = f32[3,8,16,128]{3,2,1,0:T(8,128)} copy(f32[3,8,16,128]{3,2,1,0:T(8,128)S(1)} %copy-done) | data formatting | bytes 393216
Async XLA Ops:
  48.1 0.7 %copy-start.1 = (f32[8,3]{1,0:T(8,128)S(1)}, f32[8,3]{1,0:T(8,128)}, u32[]{:S(2)}) copy-start(f32[8,3]{1,0:T(8,128)} %get-tuple-element.5) | copy-start | bytes 292
  49.4 1.7 %copy-start = (f32[3,8,16,128]{3,2,1,0:T(8,128)S(1)}, f32[3,8,16,128]{3,2,1,0:T(8,128)}, u32[]{:S(2)}) copy-start(f32[3,8,16,128]{3,2,1,0:T(8,128)} %get-tuple-element.10) | copy-start | bytes 589828

commit v4 on v3

--- a/solution.py
+++ b/solution.py
@@ -265,8 +265,8 @@
             table = jnp.zeros((8, 128), f32)
             for k in range(K):
                 for m in range(M):
-                    table = jnp.where((rows == k) & (lanes == m), par[m * K + k], table)
-            means_out[...] = table[:K, :M]
+                    table = jnp.where((rows == m) & (lanes == k), par[m * K + k], table)
+            means_out[...] = table[:M, :K]
 
     def param(n):
         one = par[n, 0:1]
@@ -469,12 +469,12 @@
     slabv = jnp.asarray(slab_vectors(nz, S, R), f32)
     vmem = pl.BlockSpec(memory_space=pltpu.VMEM)
     lanes = S * R
-    return pl.pallas_call(
+    posterior, bias_field, means = pl.pallas_call(
         functools.partial(kernel, nz, nx, nc, chunk, owners),
         out_shape=(
             jax.ShapeDtypeStruct((K, S, R, C), jnp.bfloat16),
             jax.ShapeDtypeStruct((M, S, R, C), f32),
-            jax.ShapeDtypeStruct((K, M), f32),
+            jax.ShapeDtypeStruct((M, K), f32),
         ),
         in_specs=[pl.BlockSpec(memory_space=pl.ANY)] * 7,
         out_specs=(vmem, vmem, vmem),
@@ -513,6 +513,7 @@
             collective_id=0, has_side_effects=True, vmem_limit_bytes=65400 * 1024
         ),
     )(image, brain_mask, labels, ana, syn, rowm, slabv)
+    return posterior, bias_field, means.T
 
 
 def solution(mesh):

time: 52 us -> 51.2 us (0.985)
  local copies, waits for them, and re-layouts: 3.71 us -> 2.97 us
    pallas_call x1 -> x0, local copies, waits for them, and re-layouts: 0.65 us -> none  [local(): pl.pallas_call(functools.partial(kernel, nz, nx, nc, chunk, owners), out_...]
    unnamed x6 -> x7, local copies, waits for them, and re-layouts: 3.06 us -> 2.97 us
where the time goes in v4:
time: 51.2 us; the launch traced here: 51 us
  Pallas kernels  47.4 us (93%)
  local copies, waits for them, and re-layouts  2.97 us (6%)
  between operations  0.65 us (1%)
    pallas_call x1, Pallas kernels, local(): pl.pallas_call(functools.partial(kernel, nz, nx, nc, chunk, owners), out_...  47.4 us
    unnamed x7, local copies, waits for them, and re-layouts  2.97 us

profile of v4, /device:TPU:0, one launch (start us, length us, event | category | flops | bytes accessed | tf_op | source)
XLA Modules:
  0.0 51.0 jit_solution(17128469150824888)
XLA Ops:
  0.6 47.4 %shard_map.94 = (bf16[8,8,16,128]{3,2,1,0:T(8,128)(2,1)}, f32[3,8,16,128]{3,2,1,0:T(8,128)}, f32[3,8]{1,0:T(4,128)}) custom-call(f32[3,8,16,128]{3,2,1,0:T(8,128)} %image_h.1, s32[8,16,128]{2,1,0:T(8,128)} %mask_h.1, s32[8,16,128]{2,1,0:T(8,128)} %labels_h.1, f32[2,40,128]{2,1,0:T(8,128)} %constant.8.clone.ana_h, f32[2,40,128]{2,1,0:T(8,128)} %constant.9.clone.syn_h, ...), custom_call_target="tpu_custom_call" | custom-call | tf_op jit(solution)/shard_map/pallas_call | solution.py:472
  48.1 0.0 copy-start
  48.1 1.7 %copy.13 = bf16[8,8,16,128]{3,2,1,0:T(8,128)(2,1)} copy(bf16[8,8,16,128]{3,2,1,0:T(8,128)(2,1)} %get-tuple-element.12) | data formatting | bytes 524288
  49.8 0.0 copy-done
  49.8 0.0 copy-start.1
  49.8 0.7 %copy.14 = f32[3,8,16,128]{3,2,1,0:T(8,128)} copy(f32[3,8,16,128]{3,2,1,0:T(8,128)S(1)} %copy-done) | data formatting | bytes 393216
  50.5 0.0 copy-done.1
  50.5 0.6 %copy.15 = f32[8,3]{0,1:T(4,128)} copy(f32[8,3]{0,1:T(4,128)S(1)} %bitcast.1) | data formatting | bytes 192
Async XLA Ops:
  48.1 1.7 %copy-start = (f32[3,8,16,128]{3,2,1,0:T(8,128)S(1)}, f32[3,8,16,128]{3,2,1,0:T(8,128)}, u32[]{:S(2)}) copy-start(f32[3,8,16,128]{3,2,1,0:T(8,128)} %get-tuple-element.13) | copy-start | bytes 589828
  49.8 0.7 %copy-start.1 = (f32[3,8]{1,0:T(4,128)S(1)}, f32[3,8]{1,0:T(4,128)}, u32[]{:S(2)}) copy-start(f32[3,8]{1,0:T(4,128)} %get-tuple-element.8) | copy-start | bytes 292
